TPU v7x, 256 devices: a whole 4x4x8 slice. The times are simulated.
256 devices in a mesh: panel: 32 (over z_hi, y, core), tile: 8 (over z_lo, x).
Axes of the slice: x: 4, y: 4, z: 8 (z_hi: 4, z_lo: 2; z = z_hi * 2 + z_lo), core: 2. Of those that a mesh axis runs over, the one named last changes fastest.
Arguments:
- velocity: bfloat16 [4096, 3, 2, 4096], P('tile', None, None, 'panel'), may hold values from -6 to 6
- elevation: bfloat16 [4096, 2, 4096], P('tile', None, 'panel'), may hold values from -6 to 6
- panel_area: float32 [4096], P('panel'), may hold values from 0.5 to 2
- normal: float32 [4096], P('panel'), may hold values from -1 to 1
- block_map: int32 [4096], P('panel'), may hold values from 0 to 15
- waterline: int32 [4096], P('panel'), may hold values 0 or 1
- heading: int32 [4096], replicated, may hold values from 0 to 7
- section: float32 [16], replicated, may hold values from 0.5 to 2
- heading_table: float32 [8, 8], replicated, may hold values from 0.5 to 1.5
Outputs:
- qtf: float32 [4096, 2, 4096], P('panel', None, 'tile')
All inputs are finite; a program needn't handle non-finite values. No bound on the sum of `waterline` on one device may be relied on, other than what follows from the above.
Results may differ from a plain program's by a relative error of at most 0.0003.
Values may be sent and summed in bfloat16 or wider, within the bound.
A program may use at most 128 MiB of HBM per device.

v0:
```python
import math

import jax
import jax.numpy as jnp
from jax import lax
from jax.sharding import PartitionSpec as P


def panel_weights(panel_area, normal, block_map, waterline, section, norm_scale):
    sections = jnp.arange(section.shape[0], dtype=jnp.int32)
    section_gain = jnp.sum(
        jnp.where(
            block_map[None, :] == sections[:, None],
            section[:, None],
            jnp.zeros_like(section[:, None]),
        ),
        axis=0,
    )
    mode_value = normal * section_gain * norm_scale
    pressure = -0.5 * panel_area * mode_value
    water_line = 0.5 * waterline.astype(jnp.float32) * mode_value
    return jnp.stack([pressure, pressure, pressure, water_line], axis=0)


def weighted_side(fields, weights):
    direct = fields.astype(jnp.float32) * weights[None, :, None, :]
    rotated = jnp.stack([-direct[:, :, 1], direct[:, :, 0]], axis=2)
    return jnp.stack([direct, rotated], axis=0)


def per_device(
    velocity, elevation, panel_area, normal, block_map, waterline, heading, section, heading_table
):
    own_rows = velocity.shape[0]
    panels = velocity.shape[3]
    norm_scale = 1.0 / math.sqrt(panels * lax.axis_size("panel"))
    fields = jnp.concatenate([velocity, elevation[:, None]], axis=1)
    weights = panel_weights(panel_area, normal, block_map, waterline, section, norm_scale)
    right_side = weighted_side(fields, weights).reshape(2 * own_rows, -1)
    out_rows = heading.shape[0] // lax.axis_size("panel")
    gathered = lax.all_gather(fields, "tile", axis=0, tiled=True)
    left_side = gathered.reshape(gathered.shape[0], -1).astype(jnp.float32)
    product = lax.dot_general(
        left_side,
        right_side,
        (((1,), (1,)), ((), ())),
        precision=lax.Precision.HIGHEST,
        preferred_element_type=jnp.float32,
    )
    summed = lax.psum_scatter(
        product.reshape(gathered.shape[0], 2, own_rows), "panel", scatter_dimension=0, tiled=True
    )
    kinds = jnp.arange(heading_table.shape[0], dtype=jnp.int32)
    head_rows = lax.dynamic_slice_in_dim(heading, lax.axis_index("panel") * out_rows, out_rows, 0)
    head_cols = lax.dynamic_slice_in_dim(heading, lax.axis_index("tile") * own_rows, own_rows, 0)
    onehot_rows = (head_rows[:, None] == kinds[None, :]).astype(jnp.float32)
    onehot_cols = (kinds[:, None] == head_cols[None, :]).astype(jnp.float32)
    factor = jnp.dot(
        jnp.dot(onehot_rows, heading_table, precision=lax.Precision.HIGHEST),
        onehot_cols,
        precision=lax.Precision.HIGHEST,
    )
    return summed * factor[:, None, :]


def solution(mesh):
    placed = (
        P("tile", None, None, "panel"),
        P("tile", None, "panel"),
        P("panel"),
        P("panel"),
        P("panel"),
        P("panel"),
        P(),
        P(),
        P(),
    )
    return jax.shard_map(
        per_device, mesh=mesh, in_specs=placed, out_specs=P("panel", None, "tile"), check_vma=False
    )
```

profile of v0, /device:TPU:43, one launch (start us, length us, event | category | flops | bytes accessed | tf_op | source)
XLA Modules:
  0.0 312.5 jit_solution(12184072532176741156)
XLA Ops:
  6.5 0.0 copy-start
  6.5 0.0 all-gather.2.cloned.1.call-start
  6.5 1.2 copy.28
  7.8 0.0 copy-start.4
  7.8 0.0 copy-start.5
  7.8 0.0 copy-start.1
  7.8 0.0 copy-start.2
  7.8 0.0 copy-start.3
  7.9 1.0 copy.27
  8.9 1.1 pad_maximum_fusion
  9.9 0.0 all-gather.2.cloned.1.call-update
  9.9 0.0 reduce-scatter.2.cloned.1.call-start
  10.0 0.0 copy-done.4
  10.0 0.0 copy-done.5
  10.0 0.1 select_reduce_fusion
  10.1 0.0 copy-done.1
  10.1 0.0 copy-done.2
  10.1 0.0 copy-done.3
  10.2 0.2 convert_multiply_fusion
  10.3 0.1 slice_negate_fusion
  10.5 0.1 maximum_bitcast_fusion
  10.6 1.5 convert_multiply_fusion.1
  12.2 92.7 %all-gather.2.cloned.1.call-done = bf16[4096,4,2,128]{3,0,2,1:T(8,128)(2,1)} async-done(((bf16[512,4,2,128]{3,0,2,1:T(8,128)(2,1)}), bf16[4096,4,2,128]{3,0,2,1:T(8,128)(2,1)}) %all-gather.2.cloned.1.call-update) | async-done | bytes 8388624 | tf_op jit(solution)/shard_map/all_gather | solution.py:41
  104.9 31.2 %convolution_bitcast_fusion = f32[4096,2,512]{2,0,1:T(8,128)} fusion(bf16[4096,4,2,128]{3,0,2,1:T(8,128)(2,1)} %all-gather.2.cloned.1.call-done, f32[1,512,4,2,128]{4,1,3,2,0:T(8,128)S(1)} %maximum_bitcast_fusion, f32[1,512,4,2,128]{4,1,3,2,0:T(8,128)} %convert_multiply_fusion.1), kind=kOutput, calls=%fused_computation | convolution fusion | flops 51540656128 | bytes 29360128 | tf_op jit(solution)/shard_map/dot_general | solution.py:43
  136.1 0.0 reduce-scatter.2.cloned.1.call-update
  136.1 0.8 dynamic_slice.6
  136.9 0.8 dynamic_slice.7
  137.7 0.0 copy-done
  137.7 0.2 fusion.4
  137.9 0.2 fusion.6
  138.1 165.2 %reduce-scatter.2.cloned.1.call-done = f32[128,2,512]{2,0,1:T(8,128)} async-done(((f32[4096,2,512]{2,0,1:T(8,128)}), f32[128,2,512]{2,0,1:T(8,128)}) %reduce-scatter.2.cloned.1.call-update) | async-done | bytes 524304 | tf_op jit(solution)/shard_map/reduce_scatter | solution.py:50
  303.3 1.1 broadcast_multiply_fusion
  304.5 1.2 copy.19
  (2 shorter events, 0.0 us)
Async XLA Ops:
  6.5 131.1 %copy-start = (f32[8,8]{1,0:T(8,128)S(1)}, f32[8,8]{1,0:T(8,128)}, u32[]{:S(2)}) copy-start(f32[8,8]{1,0:T(8,128)} %param.17) | copy-start | bytes 772
  6.5 98.3 %all-gather.2.cloned.1.call-start = ((), (), s32[]{:S(2)}) async-start(), calls=%async_computation.1 | async-start | bytes 9437184 | tf_op jit(solution)/shard_map/all_gather | solution.py:41
  7.8 2.2 copy-start.4
  7.8 2.2 copy-start.5
  7.8 2.3 copy-start.1
  7.8 2.3 copy-start.2
  7.8 2.3 copy-start.3
  9.9 293.4 %reduce-scatter.2.cloned.1.call-start = ((), (), s32[]{:S(2)}) async-start(), calls=%async_computation.2 | async-start | bytes 17301504 | tf_op jit(solution)/shard_map/reduce_scatter | solution.py:50
Sparse Core Ops, SparseCore 0:
  10.1 94.7 all-gather.1
  136.3 167.0 reduce-scatter.1
where the time goes:
time: 315 us; the launch traced here: 313 us
  waiting for transfers between devices  258 us (82%)
  matrix products  31.7 us (10%)
  between operations  13.5 us (4%)
  local copies, waits for them, and re-layouts  5.02 us (2%)
  other arithmetic  4.26 us (1%)
    reduce_scatter x1, waiting for transfers between devices, per_device(): lax.psum_scatter(product.reshape(gathered.shape[0], 2, own_rows), 'panel'...  165 us
    all_gather x1, waiting for transfers between devices, per_device(): gathered = lax.all_gather(fields, 'tile', axis=0, tiled=True)  92.7 us
    dot_general x1, matrix products, per_device(): lax.dot_general(left_side, right_side, (((1,), (1,)), ((), ())), precisio...  31.2 us
  transfers between devices with their start and end apart: 2, of which 2 were waited for; matrix products, arithmetic and copies ran while one was open for 1% of the time, Pallas kernels for 0%

commit v1 on v0

v1 whole, which is shorter than its diff:
```python
import functools
import math

import jax
import jax.numpy as jnp
from jax import lax
from jax.experimental import pallas as pl
from jax.experimental.pallas import tpu as pltpu
from jax.sharding import PartitionSpec as P

MESH = pl.DeviceIdType.MESH
ROWS = 512
DEPTH = 1024
COLS = 1024
BLOCK = 128
LEVELS = 32000.0


def panel_weights(panel_area, normal, block_map, waterline, section, norm_scale):
    sections = jnp.arange(section.shape[0], dtype=jnp.int32)
    section_gain = jnp.sum(
        jnp.where(
            block_map[None, :] == sections[:, None],
            section[:, None],
            jnp.zeros_like(section[:, None]),
        ),
        axis=0,
    )
    mode_value = normal * section_gain * norm_scale
    pressure = -0.5 * panel_area * mode_value
    water_line = 0.5 * waterline.astype(jnp.float32) * mode_value
    return jnp.stack([pressure, pressure, pressure, water_line], axis=0)


def quantize(value):
    tiles = value.reshape(BLOCK // 8, 8, COLS)
    top = jnp.max(jnp.abs(tiles), axis=0)
    peak = top[:, :128]
    for k in range(1, COLS // 128):
        peak = jnp.maximum(peak, top[:, k * 128 : (k + 1) * 128])
    peak = jnp.maximum(peak, 1e-30)
    inverse = jnp.concatenate([LEVELS / peak] * (COLS // 128), axis=1)
    scaled = jnp.round(tiles * inverse[None]).astype(jnp.int32)
    return scaled.reshape(BLOCK, COLS).astype(jnp.int16), peak * (1.0 / LEVELS)


def dequantize(coded, scale):
    wide = jnp.concatenate([scale] * (COLS // 128), axis=1)
    tiles = coded.astype(jnp.int32).astype(jnp.float32).reshape(BLOCK // 8, 8, COLS)
    return (tiles * wide[None]).reshape(BLOCK, COLS)


def kernel(
    field_ref, weight_ref, out_ref,
    held, across, own_hi, own_lo, across_hi, across_lo, part, core_in,
    y_out, y_out_scale, y_in, y_in_scale, z_out, z_out_scale, z_in, z_in_scale,
    total, mirror_in,
    g_send, g_recv, c_send, c_recv, y_send, y_recv, z_send, z_recv, m_send, m_recv,
):
    panel, tile = lax.axis_index("panel"), lax.axis_index("tile")
    zh, y, c = panel // 8, (panel // 2) % 4, panel % 2
    a, x = tile // 4, tile % 4

    def at(zh_, y_, c_, a_, x_):
        return (zh_ * 8 + y_ * 2 + c_, a_ * 4 + x_)

    def copy(src, dst, send, recv, device):
        return pltpu.make_async_remote_copy(
            src_ref=src, dst_ref=dst, send_sem=send, recv_sem=recv, device_id=device, device_id_type=MESH
        )

    shifts = (0, 1, 2, 2 * a, 1)
    odd = (0, 1, 0, 0, 1)
    crossed = (False, False, False, True, True)

    row_tile = panel // 4
    row_a, row_x = row_tile // 4, row_tile % 4
    shift = (row_x - x + 4) % 4
    is_own = jnp.logical_and(row_a == a, shift < 3)
    is_cross = jnp.logical_and(row_a != a, jnp.logical_or(shift == 1, shift == 2 * row_a))
    is_direct = jnp.logical_or(is_own, is_cross)
    gives = jnp.logical_or(is_cross, jnp.logical_and(row_a == a, shift == 1))
    off_diagonal = row_tile != tile

    core_mate = at(zh, y, 1 - c, a, x)
    z_mate = at(zh, y, c, 1 - a, x)
    x_mates = [at(zh, y, c, a, (x + k) % 4) for k in (1, 2, 3)]
    y_mates = [at(zh, (y + k) % 4, c, a, x) for k in (1, 2, 3)]
    zh_mates = [at((zh + k) % 4, y, c, a, x) for k in (1, 2, 3)]
    far_mates = [at((zh + k) % 4, y, c, 1 - a, x) for k in (1, 2, 3)]
    mirrors = [(tile * 4 + q, row_tile) for q in range(4)]

    barrier = pltpu.get_barrier_semaphore()
    always = [core_mate, z_mate] + x_mates + y_mates + zh_mates + far_mates
    for mate in always:
        pl.semaphore_signal(barrier, inc=1, device_id=mate, device_id_type=MESH)

    @pl.when(off_diagonal)
    def _():
        for mate in mirrors:
            pl.semaphore_signal(barrier, inc=1, device_id=mate, device_id_type=MESH)
        pl.semaphore_wait(barrier, len(always) + len(mirrors))

    @pl.when(jnp.logical_not(off_diagonal))
    def _():
        pl.semaphore_wait(barrier, len(always))

    gathers = [
        copy(field_ref, held.at[1], g_send.at[0], g_recv.at[0], x_mates[2]),
        copy(field_ref, held.at[2], g_send.at[1], g_recv.at[1], x_mates[1]),
        copy(field_ref, across, g_send.at[2], g_recv.at[2], z_mate),
    ]
    for gather in gathers:
        gather.start()

    def right_side(src, hi, lo):
        @pl.loop(0, 4)
        def _(q):
            rows = pl.ds(pl.multiple_of(q * BLOCK, BLOCK), BLOCK)
            direct = pl.ds(pl.multiple_of(q * 2 * BLOCK, BLOCK), BLOCK)
            rotated = pl.ds(pl.multiple_of(q * 2 * BLOCK + BLOCK, BLOCK), BLOCK)
            for k in range(DEPTH // 128):
                lanes = pl.ds(k * 128, 128)
                turned = pl.ds((k ^ 1) * 128, 128)
                value = src[rows, lanes].astype(jnp.float32) * weight_ref[:, lanes]
                high = value.astype(jnp.bfloat16)
                low = (value - high.astype(jnp.float32)).astype(jnp.bfloat16)
                hi[direct, lanes] = high
                lo[direct, lanes] = low
                hi[rotated, turned] = high if k % 2 == 0 else -high
                lo[rotated, turned] = low if k % 2 == 0 else -low

    def product(p, left, hi, lo):
        @pl.loop(0, 4)
        def _(k):
            columns = pl.ds(pl.multiple_of(k * 256, 256), 256)
            for r in range(2):
                rows = pl.ds(r * 256, 256)
                value = lax.dot_general(
                    left[rows, :], hi[columns, :], (((1,), (1,)), ((), ())), preferred_element_type=jnp.float32
                )
                value += lax.dot_general(
                    left[rows, :], lo[columns, :], (((1,), (1,)), ((), ())), preferred_element_type=jnp.float32
                )
                part[p, rows, columns] = value

    def core_copies(p):
        out = []
        for low in range(2):
            rows = pl.ds(pl.multiple_of((1 - c) * BLOCK + low * 2 * BLOCK, BLOCK), BLOCK)
            out.append(
                copy(part.at[p, rows], core_in.at[p, low], c_send.at[p, low], c_recv.at[p, low], core_mate)
            )
        return out

    def mine(p, low):
        return pl.ds(pl.multiple_of(c * BLOCK + low * 2 * BLOCK, BLOCK), BLOCK)

    def y_half(p):
        return (x + odd[p]) % 2

    def y_copies(p, low):
        target = y_half(p) * 2 + low
        slot = (y - target + 4) % 4 - 1
        device = at(zh, target, c, a, x)
        return [
            copy(y_out.at[p, low], y_in.at[p, slot], y_send.at[p, low, 0], y_recv.at[p, slot, 0], device),
            copy(y_out_scale.at[p, low], y_in_scale.at[p, slot], y_send.at[p, low, 1], y_recv.at[p, slot, 1], device),
        ]

    def start_core(p):
        for item in core_copies(p):
            item.start()

    def start_y(p):
        for low, item in enumerate(core_copies(p)):
            item.wait_recv()
            value = part[p, mine(p, low), :] + core_in[p, low]
            local = y_half(p) * 2 + low == y

            @pl.when(local)
            def _(value=value, low=low):
                part[p, mine(p, low), :] = value

            @pl.when(jnp.logical_not(local))
            def _(value=value, low=low):
                y_out[p, low], y_out_scale[p, low] = quantize(value)
                for each in y_copies(p, low):
                    each.start()

    def z_target(p):
        return a * 2 + ((x + shifts[p]) % 4) // 2

    def z_copies(p):
        device = at(z_target(p), y, c, 1 - a if crossed[p] else a, x)
        return [
            copy(z_out.at[p], z_in.at[zh], z_send.at[p, 0], z_recv.at[zh, 0], device),
            copy(z_out_scale.at[p], z_in_scale.at[zh], z_send.at[p, 1], z_recv.at[zh, 1], device),
        ]

    def start_z(p):
        @pl.when(y_half(p) == y // 2)
        def _():
            low = y % 2
            value = part[p, mine(p, low), :]
            for slot in range(3):
                for k, (src, dst) in enumerate(
                    ((y_out.at[p, 0], y_in.at[p, slot]), (y_out_scale.at[p, 0], y_in_scale.at[p, slot]))
                ):
                    copy(src, dst, y_send.at[p, 0, k], y_recv.at[p, slot, k], y_mates[0]).wait_recv()
                value += dequantize(y_in[p, slot], y_in_scale[p, slot])

            def send():
                z_out[p], z_out_scale[p] = quantize(value)
                for each in z_copies(p):
                    each.start()

            if crossed[p]:
                send()
            else:
                local = z_target(p) == zh

                @pl.when(local)
                def _():
                    total[...] = value

                @pl.when(jnp.logical_not(local))
                def _():
                    send()

    right_side(field_ref, own_hi, own_lo)
    product(0, field_ref, own_hi, own_lo)
    start_core(0)
    held[0] = field_ref[...]
    start_y(0)
    gathers[0].wait_recv()
    product(1, held.at[1], own_hi, own_lo)
    start_core(1)
    gathers[2].wait_recv()
    right_side(across, across_hi, across_lo)
    start_y(1)
    product(4, held.at[1], across_hi, across_lo)
    start_core(4)
    start_z(0)
    start_y(4)
    gathers[1].wait_recv()
    product(2, held.at[2], own_hi, own_lo)
    start_core(2)
    product(3, held.at[2 * a], across_hi, across_lo)
    start_core(3)
    start_y(2)
    start_y(3)
    start_z(1)
    start_z(4)
    start_z(2)
    start_z(3)

    def wait_z(source):
        for k, (src, dst) in enumerate(((z_out.at[0], z_in.at[source]), (z_out_scale.at[0], z_in_scale.at[source]))):
            copy(src, dst, z_send.at[0, k], z_recv.at[source, k], zh_mates[0]).wait_recv()

    @pl.when(is_own)
    def _():
        for k in range(1, 4):
            source = (zh + k) % 4
            wait_z(source)
            total[...] += dequantize(z_in[source], z_in_scale[source])

    @pl.when(is_cross)
    def _():
        for source in range(4):
            wait_z(source)
            value = dequantize(z_in[source], z_in_scale[source])
            total[...] = value if source == 0 else total[...] + value

    def mirror_copies():
        slot = panel % 4
        return [
            copy(
                total.at[:, pl.ds(q * 256, 256)], mirror_in.at[slot], m_send.at[q], m_recv.at[slot], mirrors[q]
            )
            for q in range(4)
        ]

    @pl.when(gives)
    def _():
        for each in mirror_copies():
            each.start()

    @pl.when(is_direct)
    def _():
        for q in range(4):
            out_ref[:, q * 128 : (q + 1) * 128] = total[:, q * 256 : q * 256 + 128]
            out_ref[:, 512 + q * 128 : 512 + (q + 1) * 128] = total[:, q * 256 + 128 : (q + 1) * 256]

    @pl.when(jnp.logical_not(is_direct))
    def _():
        for q in range(4):
            copy(
                total.at[:, pl.ds(q * 256, 256)], mirror_in.at[q], m_send.at[q], m_recv.at[q], mirrors[q]
            ).wait_recv()
            out_ref[:, q * 128 : (q + 1) * 128] = mirror_in[q, :, :128].T
            out_ref[:, 512 + q * 128 : 512 + (q + 1) * 128] = -mirror_in[q, :, 128:].T

    for gather in gathers:
        gather.wait_send()
    for p in range(5):
        for low, item in enumerate(core_copies(p)):
            item.wait_send()

            @pl.when(y_half(p) * 2 + low != y)
            def _(p=p, low=low):
                for each in y_copies(p, low):
                    each.wait_send()

        sends = y_half(p) == y // 2
        if not crossed[p]:
            sends = jnp.logical_and(sends, z_target(p) != zh)

        @pl.when(sends)
        def _(p=p):
            for each in z_copies(p):
                each.wait_send()

    @pl.when(gives)
    def _():
        for each in mirror_copies():
            each.wait_send()


def reduced_product(fields, weights):
    vmem, f32, bf16, i16 = pltpu.VMEM, jnp.float32, jnp.bfloat16, jnp.int16
    dma = pltpu.SemaphoreType.DMA
    return pl.pallas_call(
        kernel,
        out_shape=jax.ShapeDtypeStruct((BLOCK, COLS), f32),
        in_specs=[pl.BlockSpec(memory_space=vmem)] * 2,
        out_specs=pl.BlockSpec(memory_space=vmem),
        scratch_shapes=[
            vmem((3, ROWS, DEPTH), bf16), vmem((ROWS, DEPTH), bf16),
            vmem((COLS, DEPTH), bf16), vmem((COLS, DEPTH), bf16),
            vmem((COLS, DEPTH), bf16), vmem((COLS, DEPTH), bf16),
            vmem((5, ROWS, COLS), f32), vmem((5, 2, BLOCK, COLS), f32),
            vmem((5, 2, BLOCK, COLS), i16), vmem((5, 2, 8, 128), f32),
            vmem((5, 3, BLOCK, COLS), i16), vmem((5, 3, 8, 128), f32),
            vmem((5, BLOCK, COLS), i16), vmem((5, 8, 128), f32),
            vmem((4, BLOCK, COLS), i16), vmem((4, 8, 128), f32),
            vmem((BLOCK, COLS), f32), vmem((4, BLOCK, 256), f32),
            dma((3,)), dma((3,)), dma((5, 2)), dma((5, 2)),
            dma((5, 2, 2)), dma((5, 3, 2)), dma((5, 2)), dma((4, 2)), dma((4,)), dma((4,)),
        ],
        compiler_params=pltpu.CompilerParams(
            collective_id=0, has_side_effects=True, vmem_limit_bytes=56 * 2**20
        ),
        cost_estimate=pl.CostEstimate(
            flops=2 * 2 * 5 * ROWS * COLS * DEPTH, bytes_accessed=2 * ROWS * DEPTH * 2, transcendentals=0
        ),
    )(fields, weights)


def per_device(
    velocity, elevation, panel_area, normal, block_map, waterline, heading, section, heading_table
):
    own_rows = velocity.shape[0]
    panels = velocity.shape[3]
    norm_scale = 1.0 / math.sqrt(panels * lax.axis_size("panel"))
    fields = jnp.concatenate([velocity, elevation[:, None]], axis=1).reshape(own_rows, -1)
    weights = panel_weights(panel_area, normal, block_map, waterline, section, norm_scale)
    weights = jnp.broadcast_to(weights[:, None, :], (4, 2, panels)).reshape(1, -1)
    out_rows = heading.shape[0] // lax.axis_size("panel")
    summed = reduced_product(fields, weights).reshape(out_rows, 2, own_rows)
    kinds = jnp.arange(heading_table.shape[0], dtype=jnp.int32)
    head_rows = lax.dynamic_slice_in_dim(heading, lax.axis_index("panel") * out_rows, out_rows, 0)
    head_cols = lax.dynamic_slice_in_dim(heading, lax.axis_index("tile") * own_rows, own_rows, 0)
    onehot_rows = (head_rows[:, None] == kinds[None, :]).astype(jnp.float32)
    onehot_cols = (kinds[:, None] == head_cols[None, :]).astype(jnp.float32)
    factor = jnp.dot(
        jnp.dot(onehot_rows, heading_table, precision=lax.Precision.HIGHEST),
        onehot_cols,
        precision=lax.Precision.HIGHEST,
    )
    return summed * factor[:, None, :]


def solution(mesh):
    placed = (
        P("tile", None, None, "panel"),
        P("tile", None, "panel"),
        P("panel"),
        P("panel"),
        P("panel"),
        P("panel"),
        P(),
        P(),
        P(),
    )
    return jax.shard_map(
        per_device, mesh=mesh, in_specs=placed, out_specs=P("panel", None, "tile"), check_vma=False
    )
```

time: 315 us -> 138 us (0.44)
  the two profiles are of different devices: /device:TPU:43 before, /device:TPU:155 now
where the time goes in v1:
time: 138 us
  Pallas kernels  128 us (93%)
  local copies, waits for them, and re-layouts  5.76 us (4%)
  other arithmetic  3.83 us (3%)
    pallas_call x1, Pallas kernels, reduced_product(): pl.pallas_call(kernel, out_shape=jax.ShapeDtypeStruct((BLOCK, COLS), f32)...  128 us

profile of v1, /device:TPU:155, one launch (start us, length us, event | category | flops | bytes accessed | tf_op | source)
XLA Modules:
  0.0 138.1 jit_solution(17979515745026312437)
XLA Ops:
  0.0 0.0 copy-start
  0.0 2.6 %pad_maximum_fusion = bf16[512,4,2,128]{3,2,1,0:T(2,128)(2,1)S(1)} fusion(bf16[512,1,2,128]{3,2,1,0:T(2,128)(2,1)} %bitcast.10, bf16[512,3,2,128]{3,2,1,0:T(2,128)(2,1)} %param.9), kind=kLoop, calls=%fused_computation | loop fusion | flops 524288 | bytes 2097152 | tf_op jit(solution)/shard_map/concatenate | solution.py:367
  2.7 0.0 copy-start.4
  2.7 0.0 copy-start.5
  2.7 1.6 %reshape.15.field_ref = bf16[512,1024]{1,0:T(8,128)(2,1)} reshape(bf16[512,4,2,128]{3,2,1,0:T(2,128)(2,1)S(1)} %pad_maximum_fusion) | data formatting | bytes 2097152 | tf_op jit(solution)/shard_map/reshape | solution.py:367
  4.2 0.0 copy-done.4
  4.2 0.0 copy-done.5
  4.2 0.0 copy-start.1
  4.2 0.0 copy-start.2
  4.2 0.0 copy-start.3
  4.3 0.1 select_reduce_fusion
  4.3 0.5 copy-done.1
  4.9 0.0 copy-done.2
  4.9 0.0 copy-done.3
  4.9 0.6 broadcast_in_dim.23
  5.5 127.9 %shard_map.91 = f32[128,1024]{1,0:T(8,128)} custom-call(bf16[512,1024]{1,0:T(8,128)(2,1)} %reshape.15.field_ref, f32[1,1024]{1,0:T(1,128)} %bitcast.11), custom_call_target="tpu_custom_call" | custom-call | flops 10737418240 | bytes 2097152 | tf_op jit(solution)/shard_map/pallas_call | solution.py:334
  133.5 1.5 %reshape.17 = f32[128,2,512]{2,1,0:T(2,128)S(1)} reshape(f32[128,1024]{1,0:T(8,128)} %shard_map.91) | data formatting | bytes 1048576 | tf_op jit(solution)/shard_map/reshape | solution.py:371
  135.0 0.8 dynamic_slice.6
  135.7 0.0 copy-done
  135.8 0.2 fusion
  136.0 0.8 dynamic_slice.7
  136.8 0.2 fusion.2
  137.0 1.1 broadcast_multiply_fusion
  (2 shorter events, 0.0 us)
Async XLA Ops:
  0.0 135.8 %copy-start = (f32[8,8]{1,0:T(8,128)S(1)}, f32[8,8]{1,0:T(8,128)}, u32[]{:S(2)}) copy-start(f32[8,8]{1,0:T(8,128)} %param.17) | copy-start | bytes 772
  2.7 1.6 %copy-start.4 = (f32[16]{0:T(128)S(1)}, f32[16]{0:T(128)}, u32[]{:S(2)}) copy-start(f32[16]{0:T(128)} %param.16) | copy-start | bytes 196
  2.7 1.6 %copy-start.5 = (s32[128]{0:T(128)S(1)}, s32[128]{0:T(128)}, u32[]{:S(2)}) copy-start(s32[128]{0:T(128)} %param.13) | copy-start | bytes 1540
  4.2 0.7 copy-start.1
  4.2 0.7 copy-start.2
  4.2 0.7 copy-start.3

commit v2 on v0

v2 whole, which is shorter than its diff:
```python
import functools
import math

import jax
import jax.numpy as jnp
from jax import lax
from jax.experimental import pallas as pl
from jax.experimental.pallas import tpu as pltpu
from jax.sharding import PartitionSpec as P

MESH = pl.DeviceIdType.MESH
ROWS = 512
DEPTH = 1024
COLS = 1024
HALF = 512
BLOCK = 128
LEVELS = 32000.0


def across_lanes(row, width):
    return jnp.concatenate([row] * (width // 128), axis=1)


def quantize(value):
    tiles = value.reshape(BLOCK // 8, 8, HALF)
    top = jnp.max(jnp.abs(tiles), axis=0)
    peak = top[:, :128]
    for k in range(1, HALF // 128):
        peak = jnp.maximum(peak, top[:, k * 128 : (k + 1) * 128])
    peak = jnp.maximum(peak, 1e-30)
    scaled = jnp.round(tiles * across_lanes(LEVELS / peak, HALF)[None]).astype(jnp.int32)
    return scaled.reshape(BLOCK, HALF).astype(jnp.int16), peak * (1.0 / LEVELS)


def dequantize(coded, scale):
    width = coded.shape[1]
    tiles = coded.astype(jnp.int32).astype(jnp.float32).reshape(BLOCK // 8, 8, width)
    return (tiles * across_lanes(scale, width)[None]).reshape(BLOCK, width)


def kernel(
    norm_scale,
    velocity_ref, elevation_ref, area_ref, normal_ref, map_ref, line_ref, heading_ref, section_ref, table_ref,
    out_ref,
    held, relay, across, own_hi, own_lo, across_hi, across_lo, part, core_in,
    y_out, y_out_scale, y_in, y_in_scale, z_out, z_out_scale, z_in, z_in_scale,
    total, m_out, m_out_scale, m_in, m_in_scale, factor,
    g_send, g_recv, c_send, c_recv, y_send, y_recv, z_send, z_recv, m_send, m_recv,
):
    panel, tile = lax.axis_index("panel"), lax.axis_index("tile")
    zh, y, c = panel // 8, (panel // 2) % 4, panel % 2
    a, x = tile // 4, tile % 4

    def at(zh_, y_, c_, a_, x_):
        return (zh_ * 8 + y_ * 2 + c_, a_ * 4 + x_)

    def copy(src, dst, send, recv, device):
        return pltpu.make_async_remote_copy(
            src_ref=src, dst_ref=dst, send_sem=send, recv_sem=recv, device_id=device, device_id_type=MESH
        )

    shifts = (0, 1, 2, 0, 1, 2)
    crossed = (False, False, False, True, True, True)
    shared = (False, False, True, True, False, True)

    def quadrant(p, half):
        return (half + (a if crossed[p] else x // 2)) % 2

    row_tile = panel // 4
    row_a, row_x = row_tile // 4, row_tile % 4
    shift = (row_x - x + 4) % 4
    same = row_a == a
    other = jnp.logical_not(same)
    owner = [jnp.logical_and(other if crossed[p] else same, shift == shifts[p]) for p in range(6)]
    kept = (y + jnp.where(same, x // 2, row_a)) % 2
    owns_all = jnp.logical_or(owner[0], jnp.logical_or(owner[1], owner[4]))
    owns_half = jnp.logical_or(owner[2], jnp.logical_or(owner[3], owner[5]))
    off_diagonal = row_tile != tile

    core_mate = at(zh, y, 1 - c, a, x)
    z_mate = at(zh, y, c, 1 - a, x)
    ahead, behind = at(zh, y, c, a, (x + 1) % 4), at(zh, y, c, a, (x + 3) % 4)
    y_mates = [at(zh, (y + k) % 4, c, a, x) for k in (1, 2, 3)]
    zh_mates = [at((zh + k) % 4, y, c, a, x) for k in (1, 2, 3)]
    far_mates = [at((zh + k) % 4, y, c, 1 - a, x) for k in (1, 2, 3)]
    mirrors = [(tile * 4 + q, row_tile) for q in range(4)]

    barrier = pltpu.get_barrier_semaphore()
    always = [core_mate, z_mate, ahead, behind] + y_mates + zh_mates + far_mates
    for mate in always:
        pl.semaphore_signal(barrier, inc=1, device_id=mate, device_id_type=MESH)

    @pl.when(off_diagonal)
    def _():
        for mate in mirrors:
            pl.semaphore_signal(barrier, inc=1, device_id=mate, device_id_type=MESH)

    held[0, :, :768] = velocity_ref[...]
    held[0, :, 768:] = elevation_ref[...]

    @pl.when(off_diagonal)
    def _():
        pl.semaphore_wait(barrier, len(always) + len(mirrors))

    @pl.when(jnp.logical_not(off_diagonal))
    def _():
        pl.semaphore_wait(barrier, len(always))

    low, high = pl.ds(0, 256), pl.ds(256, 256)
    first, second, short = pl.ds(352, 160), pl.ds(192, 160), pl.ds(0, 192)

    def gather(k, src, dst, device):
        return copy(src, dst, g_send.at[k], g_recv.at[k], device)

    next_low = gather(0, held.at[0, low], held.at[1, low], behind)
    next_high = gather(1, held.at[0, high], held.at[1, high], behind)
    across_low = gather(2, held.at[0, low], across.at[low], z_mate)
    across_high = gather(3, held.at[0, high], across.at[high], z_mate)
    relay_first = gather(4, held.at[0, first], relay.at[pl.ds(160, 160)], ahead)
    relay_second = gather(5, held.at[0, second], relay.at[pl.ds(0, 160)], ahead)
    pass_first = gather(6, relay.at[pl.ds(160, 160)], held.at[2, first], ahead)
    pass_second = gather(7, relay.at[pl.ds(0, 160)], held.at[2, second], ahead)
    pass_short = gather(8, held.at[1, short], held.at[2, short], behind)
    for each in (next_low, across_low, relay_first, next_high, across_high, relay_second):
        each.start()

    gain = jnp.zeros((1, BLOCK), jnp.float32)
    for k in range(section_ref.shape[0]):
        gain = gain + jnp.where(map_ref[...] == k, section_ref[k], 0.0)
    mode_value = normal_ref[...] * gain * norm_scale
    pressure = -0.5 * area_ref[...] * mode_value
    water_line = 0.5 * line_ref[...].astype(jnp.float32) * mode_value

    def right_side(src, hi, lo, blocks):
        for q in blocks:
            rows = pl.ds(q * BLOCK, BLOCK)
            direct = pl.ds(q * 2 * BLOCK, BLOCK)
            rotated = pl.ds(q * 2 * BLOCK + BLOCK, BLOCK)
            for k in range(DEPTH // 128):
                lanes = pl.ds(k * 128, 128)
                turned = pl.ds((k ^ 1) * 128, 128)
                value = src[rows, lanes].astype(jnp.float32) * (pressure if k < 6 else water_line)
                upper = value.astype(jnp.bfloat16)
                lower = (value - upper.astype(jnp.float32)).astype(jnp.bfloat16)
                hi[direct, lanes] = upper
                lo[direct, lanes] = lower
                hi[rotated, turned] = upper if k % 2 == 0 else -upper
                lo[rotated, turned] = lower if k % 2 == 0 else -lower

    def core_copy(p, half, side):
        rows = pl.ds(pl.multiple_of((1 - c) * BLOCK + half * 2 * BLOCK, BLOCK), BLOCK)
        return copy(
            part.at[p, side, rows], core_in.at[p, half], c_send.at[p, half], c_recv.at[p, half], core_mate
        ) if shared[p] else copy(
            part.at[p, side, rows], core_in.at[p + 6 * side, half],
            c_send.at[p + 6 * side, half], c_recv.at[p + 6 * side, half], core_mate,
        )

    def product(p, half, side):
        left = held.at[shifts[p]]
        hi, lo = (across_hi, across_lo) if crossed[p] else (own_hi, own_lo)
        rows = pl.ds(pl.multiple_of(half * 256, 256), 256)
        columns = pl.ds(pl.multiple_of(side * HALF, HALF), HALF)
        value = lax.dot_general(
            left[rows, :], hi[columns, :], (((1,), (1,)), ((), ())), preferred_element_type=jnp.float32
        )
        value += lax.dot_general(
            left[rows, :], lo[columns, :], (((1,), (1,)), ((), ())), preferred_element_type=jnp.float32
        )
        part[p, side, rows, :] = value
        core_copy(p, half, side).start()

    def mine(half):
        return pl.ds(pl.multiple_of(c * BLOCK + half * 2 * BLOCK, BLOCK), BLOCK)

    def y_half(p):
        return (x + shifts[p]) % 2

    def slot_of(p, side):
        return p if shared[p] else p + 6 * side

    def y_copies(p, half, side):
        target = y_half(p) * 2 + half
        source = (y - target + 4) % 4 - 1
        device = at(zh, target, c, a, x)
        k = slot_of(p, side)
        return [
            copy(y_out.at[k, half], y_in.at[k, source], y_send.at[k, half, 0], y_recv.at[k, source, 0], device),
            copy(
                y_out_scale.at[k, half], y_in_scale.at[k, source],
                y_send.at[k, half, 1], y_recv.at[k, source, 1], device,
            ),
        ]

    def start_y(p, half, side):
        core_copy(p, half, side).wait_recv()
        k = slot_of(p, side)
        value = part[p, side, mine(half), :] + core_in[k, half]
        local = y_half(p) * 2 + half == y

        @pl.when(local)
        def _():
            part[p, side, mine(half), :] = value

        @pl.when(jnp.logical_not(local))
        def _():
            y_out[k, half], y_out_scale[k, half] = quantize(value)
            for each in y_copies(p, half, side):
                each.start()

    def z_target(p):
        return a * 2 + ((x + shifts[p]) % 4) // 2

    def z_copies(p, side):
        device = at(z_target(p), y, c, 1 - a if crossed[p] else a, x)
        k = slot_of(p, side)
        return [
            copy(z_out.at[k], z_in.at[side, zh], z_send.at[k, 0], z_recv.at[side, zh, 0], device),
            copy(z_out_scale.at[k], z_in_scale.at[side, zh], z_send.at[k, 1], z_recv.at[side, zh, 1], device),
        ]

    def sides(p):
        return [quadrant(p, y % 2)] if shared[p] else [0, 1]

    def start_z(p):
        @pl.when(y_half(p) == y // 2)
        def _():
            for side in sides(p):
                k = slot_of(p, side)
                value = part[p, side, mine(y % 2), :]
                for source in range(3):
                    for n, (src, dst) in enumerate(
                        ((y_out.at[k, 0], y_in.at[k, source]), (y_out_scale.at[k, 0], y_in_scale.at[k, source]))
                    ):
                        copy(src, dst, y_send.at[k, 0, n], y_recv.at[k, source, n], y_mates[0]).wait_recv()
                    value += dequantize(y_in[k, source], y_in_scale[k, source])

                def send(value=value, side=side, k=k):
                    z_out[k], z_out_scale[k] = quantize(value)
                    for each in z_copies(p, side):
                        each.start()

                if crossed[p]:
                    send()
                else:
                    local = z_target(p) == zh

                    @pl.when(local)
                    def _(value=value, side=side):
                        total[side] = value

                    @pl.when(jnp.logical_not(local))
                    def _(send=send):
                        send()

    def mirror_copies(side):
        slot = panel % 4
        out = []
        for k in range(2):
            device = (tile * 4 + side * 2 + k, row_tile)
            columns = pl.ds(k * 256, 256)
            out.append(
                copy(m_out.at[side, :, columns], m_in.at[slot], m_send.at[side, k, 0], m_recv.at[slot, 0], device)
            )
            out.append(
                copy(m_out_scale.at[side], m_in_scale.at[slot], m_send.at[side, k, 1], m_recv.at[slot, 1], device)
            )
        return out

    def finish(p):
        @pl.when(owner[p])
        def _():
            for side in [kept] if shared[p] else [0, 1]:
                value = None if crossed[p] else total[side]
                for source in range(4) if crossed[p] else [(zh + k) % 4 for k in (1, 2, 3)]:
                    for n, (src, dst) in enumerate(
                        ((z_out.at[0], z_in.at[side, source]), (z_out_scale.at[0], z_in_scale.at[side, source]))
                    ):
                        copy(src, dst, z_send.at[0, n], z_recv.at[side, source, n], zh_mates[0]).wait_recv()
                    term = dequantize(z_in[side, source], z_in_scale[side, source])
                    value = term if value is None else value + term
                total[side] = value
                if p > 0:
                    m_out[side], m_out_scale[side] = quantize(value)
                    for each in mirror_copies(side):
                        each.start()

    right_side(held.at[0], own_hi, own_lo, range(4))
    for half in range(2):
        for side in range(2):
            product(0, half, side)
            if half:
                start_y(0, 0, side)

    kinds = lax.broadcasted_iota(jnp.int32, (8, BLOCK), 0)
    pick_rows = (kinds == heading_ref[pl.ds(panel, 1), :]).astype(jnp.float32)
    for k in range(4):
        pick_columns = (kinds == heading_ref[pl.ds(tile * 4 + k, 1), :]).astype(jnp.float32)
        by_row = jnp.dot(
            table_ref[...], pick_columns, precision=lax.Precision.HIGHEST, preferred_element_type=jnp.float32
        )
        factor[:, k * BLOCK : (k + 1) * BLOCK] = lax.dot_general(
            pick_rows, by_row, (((0,), (0,)), ((), ())),
            precision=lax.Precision.HIGHEST, preferred_element_type=jnp.float32,
        )

    start_y(0, 1, 0)
    start_y(0, 1, 1)
    relay_first.wait_recv()
    pass_first.start()
    next_low.wait_recv()
    product(1, 0, 0)
    product(1, 0, 1)
    across_low.wait_recv()
    right_side(across, across_hi, across_lo, (0, 1))
    start_y(1, 0, 0)
    product(3, a, 0)
    product(4, 0, 0)
    start_y(1, 0, 1)
    start_y(3, a, 0)
    start_y(4, 0, 0)
    relay_second.wait_recv()
    pass_second.start()
    start_z(0)
    next_high.wait_recv()
    pass_short.start()
    product(1, 1, 0)
    product(1, 1, 1)
    product(4, 1, 0)
    start_y(1, 1, 0)
    start_y(1, 1, 1)
    across_high.wait_recv()
    right_side(across, across_hi, across_lo, (2, 3))
    start_y(4, 1, 0)
    product(4, 0, 1)
    product(4, 1, 1)
    product(3, 1 - a, 1)
    start_y(4, 0, 1)
    start_y(4, 1, 1)
    start_y(3, 1 - a, 1)
    pass_first.wait_recv()
    pass_second.wait_recv()
    product(2, 1, quadrant(2, 1))
    product(5, 1, quadrant(5, 1))
    start_y(2, 1, quadrant(2, 1))
    start_y(5, 1, quadrant(5, 1))
    pass_short.wait_recv()
    product(2, 0, quadrant(2, 0))
    product(5, 0, quadrant(5, 0))
    start_y(2, 0, quadrant(2, 0))
    start_y(5, 0, quadrant(5, 0))
    for p in (3, 1, 4, 2, 5):
        start_z(p)
    for p in range(6):
        finish(p)

    def put(side, k, real, imaginary):
        columns = slice(side * 256 + k * 128, side * 256 + (k + 1) * 128)
        out_ref[:, columns] = real * factor[:, columns]
        out_ref[:, 512 + columns.start : 512 + columns.stop] = imaginary * factor[:, columns]

    for side in range(2):
        direct = jnp.logical_or(owns_all, jnp.logical_and(owns_half, kept == side))

        @pl.when(direct)
        def _(side=side):
            for k in range(2):
                put(side, k, total[side, :, k * 256 : k * 256 + 128], total[side, :, k * 256 + 128 : k * 256 + 256])

    for side in range(2):
        direct = jnp.logical_or(owns_all, jnp.logical_and(owns_half, kept == side))

        @pl.when(jnp.logical_not(direct))
        def _(side=side):
            for k in range(2):
                slot = side * 2 + k
                copy(
                    m_out.at[0, :, pl.ds(0, 256)], m_in.at[slot], m_send.at[0, 0, 0], m_recv.at[slot, 0], mirrors[slot]
                ).wait_recv()
                copy(
                    m_out_scale.at[0], m_in_scale.at[slot], m_send.at[0, 0, 1], m_recv.at[slot, 1], mirrors[slot]
                ).wait_recv()
                value = dequantize(m_in[slot], m_in_scale[slot])
                put(side, k, value[:, :128].T, -value[:, 128:].T)

    for each in (
        next_low, next_high, across_low, across_high, relay_first, relay_second, pass_first, pass_second, pass_short
    ):
        each.wait_send()
    for p in range(6):
        for half in range(2):
            for side in [quadrant(p, half)] if shared[p] else [0, 1]:
                core_copy(p, half, side).wait_send()

                @pl.when(y_half(p) * 2 + half != y)
                def _(p=p, half=half, side=side):
                    for each in y_copies(p, half, side):
                        each.wait_send()

        sends = y_half(p) == y // 2
        if not crossed[p]:
            sends = jnp.logical_and(sends, z_target(p) != zh)

        @pl.when(sends)
        def _(p=p):
            for side in sides(p):
                for each in z_copies(p, side):
                    each.wait_send()

        if p > 0:
            @pl.when(owner[p])
            def _(p=p):
                for side in [kept] if shared[p] else [0, 1]:
                    for each in mirror_copies(side):
                        each.wait_send()


def reduced_product(norm_scale, *operands):
    vmem, f32, bf16, i16 = pltpu.VMEM, jnp.float32, jnp.bfloat16, jnp.int16
    dma = pltpu.SemaphoreType.DMA
    whole = pl.BlockSpec(memory_space=vmem)
    return pl.pallas_call(
        functools.partial(kernel, norm_scale),
        out_shape=jax.ShapeDtypeStruct((BLOCK, COLS), f32),
        in_specs=[whole] * 7 + [pl.BlockSpec(memory_space=pltpu.SMEM), whole],
        out_specs=whole,
        scratch_shapes=[
            vmem((3, ROWS, DEPTH), bf16), vmem((320, DEPTH), bf16), vmem((ROWS, DEPTH), bf16),
            vmem((COLS, DEPTH), bf16), vmem((COLS, DEPTH), bf16),
            vmem((COLS, DEPTH), bf16), vmem((COLS, DEPTH), bf16),
            vmem((6, 2, ROWS, HALF), f32), vmem((12, 2, BLOCK, HALF), f32),
            vmem((12, 2, BLOCK, HALF), i16), vmem((12, 2, 8, 128), f32),
            vmem((12, 3, BLOCK, HALF), i16), vmem((12, 3, 8, 128), f32),
            vmem((12, BLOCK, HALF), i16), vmem((12, 8, 128), f32),
            vmem((2, 4, BLOCK, HALF), i16), vmem((2, 4, 8, 128), f32),
            vmem((2, BLOCK, HALF), f32),
            vmem((2, BLOCK, HALF), i16), vmem((2, 8, 128), f32),
            vmem((4, BLOCK, 256), i16), vmem((4, 8, 128), f32), vmem((BLOCK, ROWS), f32),
            dma((9,)), dma((9,)), dma((12, 2)), dma((12, 2)),
            dma((12, 2, 2)), dma((12, 3, 2)), dma((12, 2)), dma((2, 4, 2)), dma((2, 2, 2)), dma((4, 2)),
        ],
        compiler_params=pltpu.CompilerParams(
            collective_id=0, has_side_effects=True, vmem_limit_bytes=56 * 2**20
        ),
        cost_estimate=pl.CostEstimate(
            flops=2 * 2 * 5 * ROWS * COLS * DEPTH, bytes_accessed=2 * ROWS * DEPTH * 2, transcendentals=0
        ),
    )(*operands)


def per_device(
    velocity, elevation, panel_area, normal, block_map, waterline, heading, section, heading_table
):
    rows, panels = velocity.shape[0], velocity.shape[3]
    norm_scale = 1.0 / math.sqrt(panels * lax.axis_size("panel"))
    summed = reduced_product(
        norm_scale,
        velocity.reshape(rows, -1), elevation.reshape(rows, -1),
        panel_area[None], normal[None], block_map[None], waterline[None],
        heading.reshape(-1, panels), section, heading_table,
    )
    return summed.reshape(-1, 2, rows)


def solution(mesh):
    placed = (
        P("tile", None, None, "panel"),
        P("tile", None, "panel"),
        P("panel"),
        P("panel"),
        P("panel"),
        P("panel"),
        P(),
        P(),
        P(),
    )
    return jax.shard_map(
        per_device, mesh=mesh, in_specs=placed, out_specs=P("panel", None, "tile"), check_vma=False
    )
```

time: 315 us -> 96.8 us (0.31)
  waiting for transfers between devices: 258 us -> 0 us
  Pallas kernels: 0 us -> 89.5 us
  matrix products: 31.7 us -> 0 us
  between operations: 13.5 us -> 0.01 us
  other arithmetic: 4.26 us -> 0 us
    reduce_scatter x1 -> x0, waiting for transfers between devices: 165 us -> none  [per_device(): lax.psum_scatter(product.reshape(gathered.shape[0], 2, own_rows), 'panel'...]
    all_gather x1 -> x0, waiting for transfers between devices: 92.7 us -> none  [per_device(): gathered = lax.all_gather(fields, 'tile', axis=0, tiled=True)]
    pallas_call x0 -> x1, Pallas kernels: none -> 89.5 us  [reduced_product(): pl.pallas_call(functools.partial(kernel, norm_scale), out_shape=jax.Shape...]
    dot_general x3 -> x0, matrix products: 31.7 us -> none  [the longest x1 31.2 us: per_device(): lax.dot_general(left_side, right_side, (((1,), (1,)), ((), ())), precisio...]
    reshape x0 -> x2, local copies, waits for them, and re-layouts: none -> 5.4 us  [the longest x1 3.13 us: per_device(): velocity.reshape(rows, -1)]
  transfers between devices with their start and end apart: 2 -> 0, of which waited for: 2 -> 0; matrix products, arithmetic and copies ran while one was open for 1% -> 0% of each run, Pallas kernels for 0% -> 0%
where the time goes in v2:
time: 96.8 us; the launch traced here: 96.6 us
  Pallas kernels  89.5 us (92%)
  local copies, waits for them, and re-layouts  7.09 us (7%)
    pallas_call x1, Pallas kernels, reduced_product(): pl.pallas_call(functools.partial(kernel, norm_scale), out_shape=jax.Shape...  89.5 us
    reshape x1, local copies, waits for them, and re-layouts, per_device(): velocity.reshape(rows, -1)  3.13 us
    reshape x1, local copies, waits for them, and re-layouts, per_device(): return summed.reshape(-1, 2, rows)  2.27 us

profile of v2, /device:TPU:43, one launch (start us, length us, event | category | flops | bytes accessed | tf_op | source)
XLA Modules:
  0.0 96.6 jit_solution(9109857508970456327)
XLA Ops:
  0.0 1.7 %copy.12 = bf16[64,8,2,128]{3,1,2,0:T(8,128)(2,1)} copy(bf16[64,8,2,128]{3,2,1,0:T(2,128)(2,1)} %bitcast.9) | data formatting | bytes 524288
  1.7 3.1 %reshape.12.velocity_ref = bf16[512,768]{1,0:T(8,128)(2,1)} reshape(bf16[512,3,2,128]{3,2,1,0:T(2,128)(2,1)} %param.9) | data formatting | bytes 1572864 | tf_op jit(solution)/shard_map/reshape | solution.py:458
  4.8 89.5 %shard_map.91 = f32[128,1024]{1,0:T(8,128)} custom-call(bf16[512,768]{1,0:T(8,128)(2,1)} %reshape.12.velocity_ref, bf16[512,256]{1,0:T(8,128)(2,1)} %bitcast.10, f32[1,128]{1,0:T(1,128)} %bitcast.12, f32[1,128]{1,0:T(1,128)} %bitcast.13, s32[1,128]{1,0:T(1,128)} %bitcast.14, s32[1,128]{1,0:T(1,128)} %bitcast.15, s32[32,128]{1,0:T(8,128)} %bitcast.11, ...), custom_call_target="tpu_custom_call" | custom-call | flops 10737418240 | bytes 2097152 | tf_op jit(solution)/shard_map/pallas_call | solution.py:422
  94.3 2.3 %reshape.15 = f32[128,2,512]{2,1,0:T(2,128)} reshape(f32[128,1024]{1,0:T(8,128)} %shard_map.91) | data formatting | bytes 1048576 | tf_op jit(solution)/shard_map/reshape | solution.py:462

commit v3 on v2

v3 whole, which is shorter than its diff:
```python
import functools
import math

import jax
import jax.numpy as jnp
from jax import lax
from jax.experimental import pallas as pl
from jax.experimental.pallas import tpu as pltpu
from jax.sharding import PartitionSpec as P

MESH = pl.DeviceIdType.MESH
ROWS = 512
DEPTH = 1024
COLS = 1024
HALF = 512
BLOCK = 128
LEVELS = 32000.0


def across_lanes(row, width):
    return jnp.concatenate([row] * (width // 128), axis=1)


def encode(ref, value):
    width = value.shape[1]
    tiles = value.reshape(BLOCK // 8, 8, width)
    top = jnp.max(jnp.abs(tiles), axis=0)
    peak = top[:, :128]
    for k in range(1, width // 128):
        peak = jnp.maximum(peak, top[:, k * 128 : (k + 1) * 128])
    exponent = jnp.ceil(jnp.log2(jnp.maximum(peak, 1e-30) * (1.0 / LEVELS)))
    scaled = jnp.round(tiles * across_lanes(jnp.exp2(-exponent), width)[None]).astype(jnp.int32)
    coded = scaled.reshape(BLOCK, width).astype(jnp.int16)
    for k in range(width // 128):
        ref[pl.ds(k * BLOCK, BLOCK), :] = coded[:, k * 128 : (k + 1) * 128]
    whole = exponent.astype(jnp.int32)
    ref[pl.ds(width, 16), :] = jnp.concatenate([whole, whole], axis=0).astype(jnp.int16)


def decode(ref, width=HALF):
    exponent = ref[pl.ds(width, 16), :].astype(jnp.int32).astype(jnp.float32)[:8]
    step = jnp.exp2(exponent)[None]
    pieces = []
    for k in range(width // 128):
        piece = ref[pl.ds(k * BLOCK, BLOCK), :].astype(jnp.int32).astype(jnp.float32)
        pieces.append((piece.reshape(BLOCK // 8, 8, 128) * step).reshape(BLOCK, 128))
    return jnp.concatenate(pieces, axis=1)


def kernel(
    norm_scale,
    velocity_ref, elevation_ref, area_ref, normal_ref, map_ref, line_ref, heading_ref, section_ref, table_ref,
    out_ref,
    wide, held, relay, across, own_hi, own_lo, across_hi, across_lo, part, core_in,
    y_out, y_in, z_out, z_in, total, m_out, m_in, factor,
    g_send, g_recv, c_send, c_recv, y_send, y_recv, z_send, z_recv, m_send, m_recv,
):
    panel, tile = lax.axis_index("panel"), lax.axis_index("tile")
    zh, y, c = panel // 8, (panel // 2) % 4, panel % 2
    a, x = tile // 4, tile % 4

    def at(zh_, y_, c_, a_, x_):
        return (zh_ * 8 + y_ * 2 + c_, a_ * 4 + x_)

    def copy(src, dst, send, recv, device):
        return pltpu.make_async_remote_copy(
            src_ref=src, dst_ref=dst, send_sem=send, recv_sem=recv, device_id=device, device_id_type=MESH
        )

    shifts = (0, 1, 2, 0, 1, 2)
    crossed = (False, False, False, True, True, True)
    shared = (False, False, True, True, False, True)

    def quadrant(p, half):
        return (half + (a if crossed[p] else x // 2)) % 2

    row_tile = panel // 4
    row_a, row_x = row_tile // 4, row_tile % 4
    shift = (row_x - x + 4) % 4
    same = row_a == a
    other = jnp.logical_not(same)
    owner = [jnp.logical_and(other if crossed[p] else same, shift == shifts[p]) for p in range(6)]
    kept = (y + jnp.where(same, x // 2, row_a)) % 2
    owns_all = jnp.logical_or(owner[0], jnp.logical_or(owner[1], owner[4]))
    owns_half = jnp.logical_or(owner[2], jnp.logical_or(owner[3], owner[5]))
    off_diagonal = row_tile != tile

    core_mate = at(zh, y, 1 - c, a, x)
    z_mate = at(zh, y, c, 1 - a, x)
    ahead, behind = at(zh, y, c, a, (x + 1) % 4), at(zh, y, c, a, (x + 3) % 4)
    y_mates = [at(zh, (y + k) % 4, c, a, x) for k in (1, 2, 3)]
    zh_mates = [at((zh + k) % 4, y, c, a, x) for k in (1, 2, 3)]
    far_mates = [at((zh + k) % 4, y, c, 1 - a, x) for k in (1, 2, 3)]
    mirrors = [(tile * 4 + q, row_tile) for q in range(4)]

    barrier = pltpu.get_barrier_semaphore()
    always = [core_mate, z_mate, ahead, behind] + y_mates + zh_mates + far_mates
    for mate in always:
        pl.semaphore_signal(barrier, inc=1, device_id=mate, device_id_type=MESH)

    @pl.when(off_diagonal)
    def _():
        for mate in mirrors:
            pl.semaphore_signal(barrier, inc=1, device_id=mate, device_id_type=MESH)

    for part_rows in range(0, ROWS, 256):
        wide[pl.ds(part_rows * 6, 1536)] = velocity_ref[pl.ds(part_rows * 6, 1536)].astype(jnp.float32)
        wide[pl.ds(ROWS * 6 + part_rows * 2, 512)] = elevation_ref[pl.ds(part_rows * 2, 512)].astype(jnp.float32)
        for k in range(8):
            if k < 6:
                rows = pl.ds(part_rows * 6 + k, 256, stride=6)
            else:
                rows = pl.ds(ROWS * 6 + part_rows * 2 + k - 6, 256, stride=2)
            held[0, pl.ds(part_rows, 256), k * 128 : (k + 1) * 128] = wide[rows, :].astype(jnp.bfloat16)

    @pl.when(off_diagonal)
    def _():
        pl.semaphore_wait(barrier, len(always) + len(mirrors))

    @pl.when(jnp.logical_not(off_diagonal))
    def _():
        pl.semaphore_wait(barrier, len(always))

    low, high = pl.ds(0, 256), pl.ds(256, 256)
    first, second, short = pl.ds(352, 160), pl.ds(192, 160), pl.ds(0, 192)

    def gather(k, src, dst, device):
        return copy(src, dst, g_send.at[k], g_recv.at[k], device)

    nexts = [
        gather(9 + q, held.at[0, pl.ds(q * BLOCK, BLOCK)], held.at[1, pl.ds(q * BLOCK, BLOCK)], behind)
        for q in range(4)
    ]
    across_low = gather(2, held.at[0, low], across.at[low], z_mate)
    across_high = gather(3, held.at[0, high], across.at[high], z_mate)
    relay_first = gather(4, held.at[0, first], relay.at[pl.ds(160, 160)], ahead)
    relay_second = gather(5, held.at[0, second], relay.at[pl.ds(0, 160)], ahead)
    pass_first = gather(6, relay.at[pl.ds(160, 160)], held.at[2, first], ahead)
    pass_second = gather(7, relay.at[pl.ds(0, 160)], held.at[2, second], ahead)
    pass_short = gather(8, held.at[1, short], held.at[2, short], behind)
    for each in (
        nexts[0], across_low, relay_first, nexts[3], nexts[1], across_high, relay_second, nexts[2]
    ):
        each.start()

    gain = jnp.zeros((1, BLOCK), jnp.float32)
    for k in range(section_ref.shape[0]):
        gain = gain + jnp.where(map_ref[...] == k, section_ref[k], 0.0)
    mode_value = normal_ref[...] * gain * norm_scale
    pressure = -0.5 * area_ref[...] * mode_value
    water_line = 0.5 * line_ref[...].astype(jnp.float32) * mode_value

    def right_side(src, hi, lo, blocks):
        for q in blocks:
            rows = pl.ds(q * BLOCK, BLOCK)
            direct = pl.ds(q * 2 * BLOCK, BLOCK)
            rotated = pl.ds(q * 2 * BLOCK + BLOCK, BLOCK)
            for k in range(DEPTH // 128):
                lanes = pl.ds(k * 128, 128)
                turned = pl.ds((k ^ 1) * 128, 128)
                value = src[rows, lanes].astype(jnp.float32) * (pressure if k < 6 else water_line)
                upper = value.astype(jnp.bfloat16)
                lower = (value - upper.astype(jnp.float32)).astype(jnp.bfloat16)
                hi[direct, lanes] = upper
                lo[direct, lanes] = lower
                hi[rotated, turned] = upper if k % 2 == 0 else -upper
                lo[rotated, turned] = lower if k % 2 == 0 else -lower

    def core_copy(p, half, side):
        rows = pl.ds(pl.multiple_of((1 - c) * BLOCK + half * 2 * BLOCK, BLOCK), BLOCK)
        return copy(
            part.at[p, side, rows], core_in.at[p, half], c_send.at[p, half], c_recv.at[p, half], core_mate
        ) if shared[p] else copy(
            part.at[p, side, rows], core_in.at[p + 6 * side, half],
            c_send.at[p + 6 * side, half], c_recv.at[p + 6 * side, half], core_mate,
        )

    def multiply(p, rows, side):
        left = held.at[shifts[p]]
        hi, lo = (across_hi, across_lo) if crossed[p] else (own_hi, own_lo)
        columns = pl.ds(pl.multiple_of(side * HALF, HALF), HALF)
        value = lax.dot_general(
            left[rows, :], hi[columns, :], (((1,), (1,)), ((), ())), preferred_element_type=jnp.float32
        )
        value += lax.dot_general(
            left[rows, :], lo[columns, :], (((1,), (1,)), ((), ())), preferred_element_type=jnp.float32
        )
        part[p, side, rows, :] = value

    def product(p, half, side):
        multiply(p, pl.ds(pl.multiple_of(half * 256, 256), 256), side)
        core_copy(p, half, side).start()

    def product_of(p, q, side):
        multiply(p, pl.ds(q * BLOCK, BLOCK), side)

        @pl.when(c != q % 2)
        def _():
            core_copy(p, q // 2, side).start()

    def mine(half):
        return pl.ds(pl.multiple_of(c * BLOCK + half * 2 * BLOCK, BLOCK), BLOCK)

    def y_half(p):
        return (x + shifts[p]) % 2

    def slot_of(p, side):
        return p if shared[p] else p + 6 * side

    def y_copies(p, half, side):
        target = y_half(p) * 2 + half
        source = (y - target + 4) % 4 - 1
        device = at(zh, target, c, a, x)
        k = slot_of(p, side)
        return copy(y_out.at[k, half], y_in.at[k, source], y_send.at[k, half], y_recv.at[k, source], device)

    def start_y(p, half, side):
        core_copy(p, half, side).wait_recv()
        k = slot_of(p, side)
        value = part[p, side, mine(half), :] + core_in[k, half]
        local = y_half(p) * 2 + half == y

        @pl.when(local)
        def _():
            part[p, side, mine(half), :] = value

        @pl.when(jnp.logical_not(local))
        def _():
            encode(y_out.at[k, half], value)
            y_copies(p, half, side).start()

    def start_y_of(p, q, side):
        @pl.when(c == q % 2)
        def _():
            start_y(p, q // 2, side)

    def z_target(p):
        return a * 2 + ((x + shifts[p]) % 4) // 2

    def z_copies(p, side):
        device = at(z_target(p), y, c, 1 - a if crossed[p] else a, x)
        k = slot_of(p, side)
        return copy(z_out.at[k], z_in.at[side, zh], z_send.at[k], z_recv.at[side, zh], device)

    def sides(p):
        return [quadrant(p, y % 2)] if shared[p] else [0, 1]

    def start_z(p, when=None):
        mine_now = y_half(p) == y // 2
        if when is not None:
            mine_now = jnp.logical_and(mine_now, when)

        @pl.when(mine_now)
        def _():
            for side in sides(p):
                k = slot_of(p, side)
                value = part[p, side, mine(y % 2), :]
                for source in range(3):
                    copy(
                        y_out.at[k, 0], y_in.at[k, source], y_send.at[k, 0], y_recv.at[k, source], y_mates[0]
                    ).wait_recv()
                    value += decode(y_in.at[k, source])

                def send(value=value, side=side, k=k):
                    encode(z_out.at[k], value)
                    z_copies(p, side).start()

                if crossed[p]:
                    send()
                else:
                    local = z_target(p) == zh

                    @pl.when(local)
                    def _(value=value, side=side):
                        total[side] = value

                    @pl.when(jnp.logical_not(local))
                    def _(send=send):
                        send()

    def mirror_copies(side):
        slot = panel % 4
        return [
            copy(
                m_out.at[side, k], m_in.at[slot], m_send.at[side, k], m_recv.at[slot],
                (tile * 4 + side * 2 + k, row_tile),
            )
            for k in range(2)
        ]

    def finish(p):
        @pl.when(owner[p])
        def _():
            for side in [kept] if shared[p] else [0, 1]:
                value = None if crossed[p] else total[side]
                for source in range(4) if crossed[p] else [(zh + k) % 4 for k in (1, 2, 3)]:
                    copy(
                        z_out.at[0], z_in.at[side, source], z_send.at[0], z_recv.at[side, source], zh_mates[0]
                    ).wait_recv()
                    term = decode(z_in.at[side, source])
                    value = term if value is None else value + term
                total[side] = value
                if p > 0:
                    for k, each in enumerate(mirror_copies(side)):
                        encode(m_out.at[side, k], value[:, k * 256 : (k + 1) * 256])
                        each.start()

    def wait_gathers_and_core():
        for each in (
            *nexts, across_low, across_high, relay_first, relay_second, pass_first, pass_second, pass_short
        ):
            each.wait_send()
        for p in range(6):
            for half in range(2):
                for side in [quadrant(p, half)] if shared[p] else [0, 1]:
                    core_copy(p, half, side).wait_send()

    def wait_y(pairs):
        for p in pairs:
            for half in range(2):
                for side in [quadrant(p, half)] if shared[p] else [0, 1]:
                    @pl.when(y_half(p) * 2 + half != y)
                    def _(p=p, half=half, side=side):
                        y_copies(p, half, side).wait_send()

    right_side(held.at[0], own_hi, own_lo, range(4))
    for half in range(2):
        for side in range(2):
            product(0, half, side)
    start_y(0, 0, 0)
    start_y(0, 0, 1)
    kinds = lax.broadcasted_iota(jnp.int32, (8, BLOCK), 0)
    pick_rows = (kinds == heading_ref[pl.ds(panel, 1), :]).astype(jnp.float32)
    for k in range(4):
        pick_columns = (kinds == heading_ref[pl.ds(tile * 4 + k, 1), :]).astype(jnp.float32)
        by_row = jnp.dot(
            table_ref[...], pick_columns, precision=lax.Precision.HIGHEST, preferred_element_type=jnp.float32
        )
        factor[:, k * BLOCK : (k + 1) * BLOCK] = lax.dot_general(
            pick_rows, by_row, (((0,), (0,)), ((), ())),
            precision=lax.Precision.HIGHEST, preferred_element_type=jnp.float32,
        )
    start_y(0, 1, 0)
    start_y(0, 1, 1)
    nexts[0].wait_recv()
    product_of(1, 0, 0)
    product_of(1, 0, 1)
    relay_first.wait_recv()
    pass_first.start()
    start_y_of(1, 0, 0)
    start_y_of(1, 0, 1)
    nexts[3].wait_recv()
    product_of(1, 3, 0)
    product_of(1, 3, 1)
    across_low.wait_recv()
    right_side(across, across_hi, across_lo, (0, 1))
    start_y_of(1, 3, 0)
    start_y_of(1, 3, 1)
    product_of(4, 0, 0)
    product_of(4, 3, 0)
    product(3, a, 0)
    start_y_of(4, 0, 0)
    start_y_of(4, 3, 0)
    relay_second.wait_recv()
    pass_second.start()
    start_y(3, a, 0)
    nexts[1].wait_recv()
    pass_short.start()
    product_of(1, 1, 0)
    product_of(1, 1, 1)
    product_of(4, 1, 0)
    start_z(0)
    start_y_of(1, 1, 0)
    start_y_of(1, 1, 1)
    start_y_of(4, 1, 0)
    start_z(1, y % 2 == c)
    nexts[2].wait_recv()
    product_of(1, 2, 0)
    product_of(1, 2, 1)
    product_of(4, 2, 0)
    across_high.wait_recv()
    right_side(across, across_hi, across_lo, (2, 3))
    start_y_of(1, 2, 0)
    start_y_of(1, 2, 1)
    product(4, 0, 1)
    start_y_of(4, 2, 0)
    product(4, 1, 1)
    product(3, 1 - a, 1)
    start_y(4, 0, 1)
    start_y(4, 1, 1)
    pass_first.wait_recv()
    pass_second.wait_recv()
    product(2, 1, quadrant(2, 1))
    start_y(3, 1 - a, 1)
    product(5, 1, quadrant(5, 1))
    pass_short.wait_recv()
    product(2, 0, quadrant(2, 0))
    start_y(2, 1, quadrant(2, 1))
    product(5, 0, quadrant(5, 0))
    start_y(5, 1, quadrant(5, 1))
    start_y(2, 0, quadrant(2, 0))
    start_y(5, 0, quadrant(5, 0))
    start_z(3, y % 2 == a)
    start_z(1, y % 2 != c)
    start_z(3, y % 2 != a)
    start_z(4)
    wait_gathers_and_core()
    finish(1)
    finish(4)
    start_z(2)
    start_z(5)
    wait_y(range(6))
    for p in (3, 2, 5, 0):
        finish(p)

    def put(side, k, real, imaginary):
        q = side * 2 + k
        scale = factor[:, q * 128 : (q + 1) * 128]
        out_ref[pl.ds(q * 2, BLOCK, stride=8), :] = real * scale
        out_ref[pl.ds(q * 2 + 1, BLOCK, stride=8), :] = imaginary * scale

    for side in range(2):
        direct = jnp.logical_or(owns_all, jnp.logical_and(owns_half, kept == side))

        @pl.when(direct)
        def _(side=side):
            for k in range(2):
                put(side, k, total[side, :, k * 256 : k * 256 + 128], total[side, :, k * 256 + 128 : k * 256 + 256])

    for side in range(2):
        direct = jnp.logical_or(owns_all, jnp.logical_and(owns_half, kept == side))

        @pl.when(jnp.logical_not(direct))
        def _(side=side):
            for k in range(2):
                slot = side * 2 + k
                copy(m_out.at[0, 0], m_in.at[slot], m_send.at[0, 0], m_recv.at[slot], mirrors[slot]).wait_recv()
                value = decode(m_in.at[slot], 256)
                put(side, k, value[:, :128].T, -value[:, 128:].T)

    for p in range(6):
        sends = y_half(p) == y // 2
        if not crossed[p]:
            sends = jnp.logical_and(sends, z_target(p) != zh)

        @pl.when(sends)
        def _(p=p):
            for side in sides(p):
                z_copies(p, side).wait_send()

        if p > 0:
            @pl.when(owner[p])
            def _(p=p):
                for side in [kept] if shared[p] else [0, 1]:
                    for each in mirror_copies(side):
                        each.wait_send()


def reduced_product(norm_scale, *operands):
    vmem, f32, bf16, i16 = pltpu.VMEM, jnp.float32, jnp.bfloat16, jnp.int16
    dma = pltpu.SemaphoreType.DMA
    whole = pl.BlockSpec(memory_space=vmem)
    return pl.pallas_call(
        functools.partial(kernel, norm_scale),
        out_shape=jax.ShapeDtypeStruct((BLOCK * COLS // 128, 128), f32),
        in_specs=[whole] * 7 + [pl.BlockSpec(memory_space=pltpu.SMEM), whole],
        out_specs=whole,
        scratch_shapes=[
            vmem((8 * ROWS, 128), f32), vmem((3, ROWS, DEPTH), bf16), vmem((320, DEPTH), bf16), vmem((ROWS, DEPTH), bf16),
            vmem((COLS, DEPTH), bf16), vmem((COLS, DEPTH), bf16),
            vmem((COLS, DEPTH), bf16), vmem((COLS, DEPTH), bf16),
            vmem((6, 2, ROWS, HALF), f32), vmem((12, 2, BLOCK, HALF), f32),
            vmem((12, 2, HALF + 16, 128), i16), vmem((12, 3, HALF + 16, 128), i16),
            vmem((12, HALF + 16, 128), i16), vmem((2, 4, HALF + 16, 128), i16),
            vmem((2, BLOCK, HALF), f32),
            vmem((2, 2, 272, 128), i16), vmem((4, 272, 128), i16), vmem((BLOCK, ROWS), f32),
            dma((13,)), dma((13,)), dma((12, 2)), dma((12, 2)),
            dma((12, 2)), dma((12, 3)), dma((12,)), dma((2, 4)), dma((2, 2)), dma((4,)),
        ],
        compiler_params=pltpu.CompilerParams(
            collective_id=0, has_side_effects=True, vmem_limit_bytes=56 * 2**20
        ),
        cost_estimate=pl.CostEstimate(
            flops=2 * 2 * 5 * ROWS * COLS * DEPTH, bytes_accessed=2 * ROWS * DEPTH * 2, transcendentals=0
        ),
    )(*operands)


def per_device(
    velocity, elevation, panel_area, normal, block_map, waterline, heading, section, heading_table
):
    rows, panels = velocity.shape[0], velocity.shape[3]
    norm_scale = 1.0 / math.sqrt(panels * lax.axis_size("panel"))
    summed = reduced_product(
        norm_scale,
        velocity.reshape(-1, panels), elevation.reshape(-1, panels),
        panel_area[None], normal[None], block_map[None], waterline[None],
        heading.reshape(-1, panels), section, heading_table,
    )
    return summed.reshape(-1, rows // 128, 2, 128).transpose(0, 2, 1, 3).reshape(-1, 2, rows)


def solution(mesh):
    placed = (
        P("tile", None, None, "panel"),
        P("tile", None, "panel"),
        P("panel"),
        P("panel"),
        P("panel"),
        P("panel"),
        P(),
        P(),
        P(),
    )
    return jax.shard_map(
        per_device, mesh=mesh, in_specs=placed, out_specs=P("panel", None, "tile"), check_vma=False
    )
```

time: 96.8 us -> 85.8 us (0.89)
  the two profiles are of different devices: /device:TPU:43 before, /device:TPU:45 now
where the time goes in v3:
time: 85.8 us; the launch traced here: 85.7 us
  Pallas kernels  83.8 us (98%)
  local copies, waits for them, and re-layouts  1.87 us (2%)
    pallas_call x1, Pallas kernels, reduced_product(): pl.pallas_call(functools.partial(kernel, norm_scale), out_shape=jax.Shape...  83.8 us
    unnamed x1, local copies, waits for them, and re-layouts  1.87 us

profile of v3, /device:TPU:45, one launch (start us, length us, event | category | flops | bytes accessed | tf_op | source)
XLA Modules:
  0.0 85.7 jit_solution(15988191366477193314)
XLA Ops:
  0.0 83.8 %shard_map.91 = f32[1024,128]{1,0:T(8,128)} custom-call(bf16[3072,128]{1,0:T(8,128)(2,1)} %bitcast.13, bf16[1024,128]{1,0:T(8,128)(2,1)} %bitcast.14, f32[1,128]{1,0:T(1,128)} %bitcast.16, f32[1,128]{1,0:T(1,128)} %bitcast.17, s32[1,128]{1,0:T(1,128)} %bitcast.18, s32[1,128]{1,0:T(1,128)} %bitcast.19, s32[32,128]{1,0:T(8,128)} %bitcast.15, f32[16]{0:T(128)} %section_ref.1, ...), custom_call_target="tpu_custom_call" | custom-call | flops 10737418240 | bytes 2097152 | tf_op jit(solution)/shard_map/pallas_call | solution.py:463
  83.8 1.9 %copy.12 = f32[128,2,512]{2,1,0:T(2,128)} copy(f32[128,2,512]{2,1,0:T(2,128)} %bitcast.12) | data formatting | bytes 1048576

commit v4 on v3

--- a/solution.py
+++ b/solution.py
@@ -245,14 +245,14 @@
     def sides(p):
         return [quadrant(p, y % 2)] if shared[p] else [0, 1]
 
-    def start_z(p, when=None):
+    def start_z(p, when=None, only=None):
         mine_now = y_half(p) == y // 2
         if when is not None:
             mine_now = jnp.logical_and(mine_now, when)
 
         @pl.when(mine_now)
         def _():
-            for side in sides(p):
+            for side in sides(p) if only is None else [only]:
                 k = slot_of(p, side)
                 value = part[p, side, mine(y % 2), :]
                 for source in range(3):
@@ -288,8 +288,8 @@
             for k in range(2)
         ]
 
-    def finish(p):
-        @pl.when(owner[p])
+    def finish(p, when=None):
+        @pl.when(owner[p] if when is None else jnp.logical_and(owner[p], when))
         def _():
             for side in [kept] if shared[p] else [0, 1]:
                 value = None if crossed[p] else total[side]
@@ -373,44 +373,50 @@
     start_y_of(1, 1, 0)
     start_y_of(1, 1, 1)
     start_y_of(4, 1, 0)
-    start_z(1, y % 2 == c)
+    early = y % 2 == c
+    late = jnp.logical_not(early)
+    start_z(1, early)
+    start_z(4, early, 0)
     nexts[2].wait_recv()
     product_of(1, 2, 0)
     product_of(1, 2, 1)
-    product_of(4, 2, 0)
     across_high.wait_recv()
     right_side(across, across_hi, across_lo, (2, 3))
+    product(3, 1 - a, 1)
     start_y_of(1, 2, 0)
     start_y_of(1, 2, 1)
+    product_of(4, 2, 0)
     product(4, 0, 1)
+    start_y(3, 1 - a, 1)
+    product(4, 1, 1)
     start_y_of(4, 2, 0)
-    product(4, 1, 1)
-    product(3, 1 - a, 1)
     start_y(4, 0, 1)
     start_y(4, 1, 1)
     pass_first.wait_recv()
     pass_second.wait_recv()
+    product(5, 1, quadrant(5, 1))
     product(2, 1, quadrant(2, 1))
-    start_y(3, 1 - a, 1)
-    product(5, 1, quadrant(5, 1))
+    start_y(5, 1, quadrant(5, 1))
     pass_short.wait_recv()
+    product(5, 0, quadrant(5, 0))
+    start_y(2, 1, quadrant(2, 1))
     product(2, 0, quadrant(2, 0))
-    start_y(2, 1, quadrant(2, 1))
-    product(5, 0, quadrant(5, 0))
-    start_y(5, 1, quadrant(5, 1))
+    start_y(5, 0, quadrant(5, 0))
     start_y(2, 0, quadrant(2, 0))
-    start_y(5, 0, quadrant(5, 0))
     start_z(3, y % 2 == a)
-    start_z(1, y % 2 != c)
+    start_z(1, jnp.logical_and(late, y % 2 == 0))
+    start_z(4, jnp.logical_and(late, y % 2 == 0), 0)
+    start_z(1, jnp.logical_and(late, y % 2 == 1))
+    start_z(4, jnp.logical_and(late, y % 2 == 1), 0)
     start_z(3, y % 2 != a)
-    start_z(4)
+    start_z(4, None, 1)
     wait_gathers_and_core()
     finish(1)
     finish(4)
+    start_z(5)
     start_z(2)
-    start_z(5)
     wait_y(range(6))
-    for p in (3, 2, 5, 0):
+    for p in (5, 2, 3, 0):
         finish(p)
 
     def put(side, k, real, imaginary):
@@ -462,7 +468,7 @@
     whole = pl.BlockSpec(memory_space=vmem)
     return pl.pallas_call(
         functools.partial(kernel, norm_scale),
-        out_shape=jax.ShapeDtypeStruct((BLOCK * COLS // 128, 128), f32),
+        out_shape=vmem((BLOCK * COLS // 128, 128), f32),
         in_specs=[whole] * 7 + [pl.BlockSpec(memory_space=pltpu.SMEM), whole],
         out_specs=whole,
         scratch_shapes=[

time: 85.8 us -> 80.3 us (0.936)
  the two profiles are of different devices: /device:TPU:45 before, /device:TPU:43 now
where the time goes in v4:
time: 80.3 us; the launch traced here: 78.9 us
  Pallas kernels  78.1 us (97%)
    pallas_call x1, Pallas kernels, reduced_product(): pl.pallas_call(functools.partial(kernel, norm_scale), out_shape=vmem((BLO...  78.1 us

profile of v4, /device:TPU:43, one launch (start us, length us, event | category | flops | bytes accessed | tf_op | source)
XLA Modules:
  0.0 78.9 jit_solution(2377311819600733602)
XLA Ops:
  0.0 78.1 %shard_map.91 = f32[1024,128]{1,0:T(8,128)S(1)} custom-call(bf16[3072,128]{1,0:T(8,128)(2,1)} %bitcast.13, bf16[1024,128]{1,0:T(8,128)(2,1)} %bitcast.14, f32[1,128]{1,0:T(1,128)} %bitcast.16, f32[1,128]{1,0:T(1,128)} %bitcast.17, s32[1,128]{1,0:T(1,128)} %bitcast.18, s32[1,128]{1,0:T(1,128)} %bitcast.19, s32[32,128]{1,0:T(8,128)} %bitcast.15, ...), custom_call_target="tpu_custom_call" | custom-call | flops 10737418240 | bytes 2097152 | tf_op jit(solution)/shard_map/pallas_call | solution.py:469
  78.1 0.8 %copy.12 = f32[128,2,512]{2,1,0:T(2,128)} copy(f32[128,2,512]{2,1,0:T(2,128)S(1)} %bitcast.12) | data formatting | bytes 1048576

commit v5 on v4

--- a/solution.py
+++ b/solution.py
@@ -103,7 +103,7 @@
         for mate in mirrors:
             pl.semaphore_signal(barrier, inc=1, device_id=mate, device_id_type=MESH)
 
-    for part_rows in range(0, ROWS, 256):
+    def lay_out(part_rows):
         wide[pl.ds(part_rows * 6, 1536)] = velocity_ref[pl.ds(part_rows * 6, 1536)].astype(jnp.float32)
         wide[pl.ds(ROWS * 6 + part_rows * 2, 512)] = elevation_ref[pl.ds(part_rows * 2, 512)].astype(jnp.float32)
         for k in range(8):
@@ -113,6 +113,8 @@
                 rows = pl.ds(ROWS * 6 + part_rows * 2 + k - 6, 256, stride=2)
             held[0, pl.ds(part_rows, 256), k * 128 : (k + 1) * 128] = wide[rows, :].astype(jnp.bfloat16)
 
+    lay_out(0)
+
     @pl.when(off_diagonal)
     def _():
         pl.semaphore_wait(barrier, len(always) + len(mirrors))
@@ -121,7 +123,7 @@
     def _():
         pl.semaphore_wait(barrier, len(always))
 
-    low, high = pl.ds(0, 256), pl.ds(256, 256)
+    low = pl.ds(0, 256)
     first, second, short = pl.ds(352, 160), pl.ds(192, 160), pl.ds(0, 192)
 
     def gather(k, src, dst, device):
@@ -132,15 +134,18 @@
         for q in range(4)
     ]
     across_low = gather(2, held.at[0, low], across.at[low], z_mate)
-    across_high = gather(3, held.at[0, high], across.at[high], z_mate)
+    third, fourth = pl.ds(256, 128), pl.ds(384, 128)
+    across_third = gather(3, held.at[0, third], across.at[third], z_mate)
+    across_fourth = gather(13, held.at[0, fourth], across.at[fourth], z_mate)
     relay_first = gather(4, held.at[0, first], relay.at[pl.ds(160, 160)], ahead)
     relay_second = gather(5, held.at[0, second], relay.at[pl.ds(0, 160)], ahead)
     pass_first = gather(6, relay.at[pl.ds(160, 160)], held.at[2, first], ahead)
     pass_second = gather(7, relay.at[pl.ds(0, 160)], held.at[2, second], ahead)
     pass_short = gather(8, held.at[1, short], held.at[2, short], behind)
-    for each in (
-        nexts[0], across_low, relay_first, nexts[3], nexts[1], across_high, relay_second, nexts[2]
-    ):
+    nexts[0].start()
+    across_low.start()
+    lay_out(256)
+    for each in (relay_first, nexts[3], nexts[1], across_third, relay_second, nexts[2], across_fourth):
         each.start()
 
     gain = jnp.zeros((1, BLOCK), jnp.float32)
@@ -307,7 +312,7 @@
 
     def wait_gathers_and_core():
         for each in (
-            *nexts, across_low, across_high, relay_first, relay_second, pass_first, pass_second, pass_short
+            *nexts, across_low, across_third, across_fourth, relay_first, relay_second, pass_first, pass_second, pass_short
         ):
             each.wait_send()
         for p in range(6):
@@ -377,11 +382,13 @@
     late = jnp.logical_not(early)
     start_z(1, early)
     start_z(4, early, 0)
+    across_third.wait_recv()
+    right_side(across, across_hi, across_lo, (2,))
     nexts[2].wait_recv()
     product_of(1, 2, 0)
     product_of(1, 2, 1)
-    across_high.wait_recv()
-    right_side(across, across_hi, across_lo, (2, 3))
+    across_fourth.wait_recv()
+    right_side(across, across_hi, across_lo, (3,))
     product(3, 1 - a, 1)
     start_y_of(1, 2, 0)
     start_y_of(1, 2, 1)
@@ -480,7 +487,7 @@
             vmem((12, HALF + 16, 128), i16), vmem((2, 4, HALF + 16, 128), i16),
             vmem((2, BLOCK, HALF), f32),
             vmem((2, 2, 272, 128), i16), vmem((4, 272, 128), i16), vmem((BLOCK, ROWS), f32),
-            dma((13,)), dma((13,)), dma((12, 2)), dma((12, 2)),
+            dma((14,)), dma((14,)), dma((12, 2)), dma((12, 2)),
             dma((12, 2)), dma((12, 3)), dma((12,)), dma((2, 4)), dma((2, 2)), dma((4,)),
         ],
         compiler_params=pltpu.CompilerParams(

time: 80.3 us -> 80.4 us (level)
  no operation moved by 1% of the time
where the time goes in v5:
time: 80.4 us; the launch traced here: 79 us
  Pallas kernels  78.2 us (97%)
    pallas_call x1, Pallas kernels, reduced_product(): pl.pallas_call(functools.partial(kernel, norm_scale), out_shape=vmem((BLO...  78.2 us

profile of v5, /device:TPU:43, one launch (start us, length us, event | category | flops | bytes accessed | tf_op | source)
XLA Modules:
  0.0 79.0 jit_solution(16191847766171593244)
XLA Ops:
  0.0 78.2 %shard_map.91 = f32[1024,128]{1,0:T(8,128)S(1)} custom-call(bf16[3072,128]{1,0:T(8,128)(2,1)} %bitcast.13, bf16[1024,128]{1,0:T(8,128)(2,1)} %bitcast.14, f32[1,128]{1,0:T(1,128)} %bitcast.16, f32[1,128]{1,0:T(1,128)} %bitcast.17, s32[1,128]{1,0:T(1,128)} %bitcast.18, s32[1,128]{1,0:T(1,128)} %bitcast.19, s32[32,128]{1,0:T(8,128)} %bitcast.15, ...), custom_call_target="tpu_custom_call" | custom-call | flops 10737418240 | bytes 2097152 | tf_op jit(solution)/shard_map/pallas_call | solution.py:476
  78.2 0.8 %copy.12 = f32[128,2,512]{2,1,0:T(2,128)} copy(f32[128,2,512]{2,1,0:T(2,128)S(1)} %bitcast.12) | data formatting | bytes 1048576
